TPU v7x, 32 devices: a whole 2x2x4 slice. The times are simulated.
32 devices in a mesh: chan: 16 (over z, x, core), tm: 2 (over y).
Axes of the slice: x: 2, y: 2, z: 4, core: 2. Of those that a mesh axis runs over, the one named last changes fastest.
Arguments:
- raw_strain: bfloat16 [2048, 16384], P('chan', 'tm'), may hold values from -6 to 6
- fir_taps: bfloat16 [64], replicated, may hold values from -0.75 to 0.75
- sources: int32 [2, 8], replicated, may hold values from 0 to 2047, as said below
Outputs:
- correlation: float32 [2, 8, 257, 2048], P(None, 'tm', None, 'chan')
Inputs may be any that keep to these rules, and one draw needn't show every extreme that they name: `sources`: the 16 entries are distinct channel indices; the first and the last channel are always among them.
All inputs are finite; a program needn't handle non-finite values.
Results may differ from a plain program's by a relative error of at most 0.0037.
Values may be sent and summed in bfloat16 or wider, within the bound.
A program may use at most 64 MiB of HBM per device.

v0:
```python
import math
import jax
import jax.numpy as jnp
from jax import lax
from jax.sharding import PartitionSpec as P

TAPS = 64
DECIM = 4
HALF_WIN = 32
LAGS = 257
HALF_LAG = 128
STEPS = 2
tile_width = 128


def shifted(x, axis, by):
    length = lax.axis_size(axis)
    pairs = [(i, i + by) for i in range(length) if 0 <= i + by < length]
    return lax.ppermute(x, axis, pairs)


def padded_2(x, sides, width):
    for axis, dim in sides:
        size, length = (lax.axis_size(axis), x.shape[dim])
        up = [(i, (i + 1) % size) for i in range(size - 1)]
        down = [(j, i) for i, j in up]
        last = lax.slice_in_dim(x, length - width, length, axis=dim)
        initial = lax.slice_in_dim(x, 0, width, axis=dim)
        before = lax.ppermute(last, axis, up)
        after = lax.ppermute(initial, axis, down)
        x = jnp.concatenate([before, x, after], axis=dim)
    return x


def filter_matrix(fir_taps, phases, guard_width):
    count = fir_taps.shape[0]
    offset = jnp.arange(tile_width + guard_width)[:, None, None]
    phase_ids = jnp.arange(phases)[None, :, None]
    column = jnp.arange(tile_width)[None, None, :]
    tap_index = count - phases * (offset - column) - phase_ids
    matches = tap_index[..., None] == jnp.arange(count)[None, None, None, :]
    weights = jnp.sum(jnp.where(matches, fir_taps.astype(jnp.float32), 0.0), axis=-1)
    return weights.astype(jnp.bfloat16).reshape((tile_width + guard_width) * phases, tile_width)


def decimate(extended, fir_taps, outputs):
    phases = DECIM
    guard_width = TAPS // DECIM
    channel_count = extended.shape[0]
    block_count = outputs // tile_width
    polyphase = extended.reshape(channel_count, outputs + guard_width, phases)
    padded = jnp.pad(polyphase, ((0, 0), (0, tile_width - guard_width), (0, 0)))
    leading = padded[:, :outputs].reshape(channel_count, block_count, tile_width, phases)
    trailing = padded[:, tile_width : tile_width + outputs].reshape(
        channel_count, block_count, tile_width, phases
    )
    blocks = jnp.concatenate([leading, trailing[:, :, :guard_width]], axis=2)
    blocks = blocks.reshape(channel_count, block_count, (tile_width + guard_width) * phases)
    result = jnp.einsum(
        "cbj,ji->cbi",
        blocks,
        filter_matrix(fir_taps, phases, guard_width),
        preferred_element_type=jnp.float32,
    )
    return result.reshape(channel_count, outputs)


def window_sums(magnitude, outputs):
    span_width = 2 * HALF_WIN
    channel_count = magnitude.shape[0]
    block_count = outputs // tile_width
    padded = jnp.pad(magnitude, ((0, 0), (0, tile_width - span_width)))
    leading = padded[:, :outputs].reshape(channel_count, block_count, tile_width)
    trailing = padded[:, tile_width : tile_width + outputs].reshape(
        channel_count, block_count, tile_width
    )
    blocks = jnp.concatenate([leading, trailing[:, :, :span_width]], axis=2)
    row_ids = jnp.arange(tile_width + span_width)[:, None]
    col_ids = jnp.arange(tile_width)[None, :]
    band = ((row_ids >= col_ids) & (row_ids <= col_ids + span_width)).astype(jnp.float32)
    sums = jnp.einsum(
        "cbj,ji->cbi",
        blocks,
        band,
        precision=lax.Precision.HIGHEST,
        preferred_element_type=jnp.float32,
    )
    return sums.reshape(channel_count, outputs)


def lag_products(extended_traces, receivers):
    length = receivers.shape[1]
    width = length + LAGS - 1

    def single(trace):
        tiled = jnp.tile(trace, LAGS + 1)[: LAGS * (width + 1)].reshape(LAGS, width + 1)
        toeplitz = tiled[::-1, :length]
        return jnp.einsum("lm,rm->lr", toeplitz, receivers, preferred_element_type=jnp.float32)

    return lax.map(single, extended_traces)


def per_device(raw_strain, fir_taps, sources):
    dec_dev = raw_strain.shape[1] // DECIM
    left_rim = shifted(raw_strain[:, raw_strain.shape[1] - TAPS :], "tm", 1)
    decimated = decimate(jnp.concatenate([left_rim, raw_strain], axis=1), fir_taps, dec_dev)
    beside_all = padded_2(decimated, (("tm", 1),), HALF_WIN)
    magnitude = jnp.abs(beside_all)
    level = window_sums(magnitude, dec_dev) / (2 * HALF_WIN + 1) + 1e-05
    white = (decimated / level).astype(jnp.bfloat16)
    channel_count = white.shape[0]
    my_block = lax.axis_index("chan")
    owner_ids = sources // channel_count
    local_rows = sources % channel_count
    traces = []
    for step_index in range(STEPS):
        picks = (local_rows[step_index][:, None] == jnp.arange(channel_count)[None, :]) & (
            owner_ids[step_index][:, None] == my_block
        )
        summed = lax.psum(
            jnp.dot(picks.astype(jnp.bfloat16), white, preferred_element_type=jnp.float32), "chan"
        )
        traces.append(summed.astype(jnp.bfloat16))
    scale = 1.0 / math.sqrt(dec_dev * lax.axis_size("tm"))
    terms = []
    for step_index in range(STEPS):
        extended = padded_2(traces[step_index], (("tm", 1),), HALF_LAG)
        terms.append(lag_products(extended, white) * scale)
    return lax.psum_scatter(jnp.stack(terms), "tm", scatter_dimension=1, tiled=True)


def solution(mesh):
    placed = (P("chan", "tm"), P(), P())
    return jax.shard_map(
        per_device,
        mesh=mesh,
        in_specs=placed,
        out_specs=P(None, "tm", None, "chan"),
        check_vma=False,
    )
```

profile of v0, /device:TPU:0, one launch (start us, length us, event | category | flops | bytes accessed | tf_op | source)
XLA Modules:
  0.0 399.5 jit_solution(1200064050294466446)
XLA Ops:
  9.8 4.9 %collective-permute-start = (bf16[128,64]{0,1:T(8,128)(2,1)S(1)}, bf16[128,64]{0,1:T(8,128)(2,1)S(1)}, u32[]{:S(2)}, u32[]{:S(2)}) collective-permute-start(bf16[128,64]{0,1:T(8,128)(2,1)S(1)} %slice.86), channel_id=1, source_target_pairs={{0,1},{2,3},{4,5},{6,7},{8,9},{10,11},{12,13},{14,15},{16,17},{18,... | collective-permute-start | bytes 49160 | tf_op jit(solution)/shard_map/ppermute | solution.py:19
  14.8 6.9 %select_reduce_fusion = bf16[144,4,128]{2,1,0:T(4,128)(2,1)S(1)} fusion(f32[64]{0:T(128)S(1)} %convert_element_type.22, s32[144,4,128]{2,1,0:T(4,128)S(1)} %iota_subtract_fusion), kind=kLoop, calls=%fused_computation.4 | loop fusion | flops 14082048 | bytes 442624 | tf_op jit(solution)/shard_map/reduce_sum | solution.py:42
  36.9 60.9 %all-reduce.8 = (bf16[8,2048]{1,0:T(8,128)(2,1)S(1)}, bf16[8,2048]{1,0:T(8,128)(2,1)S(1)}) all-reduce(f32[8,2048]{1,0:T(8,128)S(1)} %fusion.24, f32[8,2048]{1,0:T(8,128)S(1)} %fusion.21), channel_id=1, replica_groups=mesh['chan'=16,'tm'=2] {'chan'}, use_global_device_ids=true, to_apply=%region_4.5 | all-reduce | flops 32768 | bytes 196608 | tf_op jit(solution)/shard_map/psum | solution.py:120
  101.0 4.5 %collective-permute-start.5 = (bf16[8,128]{1,0:T(8,128)(2,1)S(1)}, bf16[8,128]{1,0:T(8,128)(2,1)S(1)}, u32[]{:S(2)}, u32[]{:S(2)}) collective-permute-start(bf16[8,128]{1,0:T(8,128)(2,1)S(1)} %get-tuple-element.77), channel_id=1, source_target_pairs={{0,1},{2,3},{4,5},{6,7},{8,9},{10,11},{12,13},{14,15},{16,17},{18,... | collective-permute-start | bytes 6152 | tf_op jit(solution)/shard_map/ppermute | solution.py:29
  108.1 107.8 %while.20 = (s32[]{:T(128)}, f32[8,257,128]{2,0,1:T(8,128)}, bf16[8,2304]{1,0:T(8,128)(2,1)S(1)}, bf16[128,2048]{1,0:T(8,128)(2,1)S(1)}, s32[]{:T(128)}, /*index=5*/s32[]{:T(128)}) while((s32[]{:T(128)}, f32[8,257,128]{2,0,1:T(8,128)}, bf16[8,2304]{1,0:T(8,128)(2,1)S(1)}, bf16[128,2048]{1,0:T(8,128)(2,1)S(1)}, s32[]{:T(128)}, ...), condition=%wide.region_3.4_spmd, body=%wide.region_2.3_spmd.sunk | while | flops 134742016 | bytes 14765141 | solution.py:100
  112.0 4.0 rev.8
  116.6 5.0 %dynamic_update_slice.9 = f32[8,257,128]{2,0,1:T(8,128)} dynamic-update-slice(f32[8,257,128]{2,0,1:T(8,128)} %get-tuple-element.162, f32[1,257,128]{2,0,1:T(1,128)S(1)} %copy.59, s32[]{:T(128)} %get-tuple-element.161, s32[]{:T(128)} %constant.54.clone.1..sunk, s32[]{:T(128)} %constant.54.clone.1..sunk) | dynamic-update-slice | bytes 263172 | tf_op jit(solution)/shard_map/while/body/jit(dynamic_update_index_in_dim)/dynamic_update_slice | solution.py:100
  130.1 5.0 %dynamic_update_slice.9 = f32[8,257,128]{2,0,1:T(8,128)} dynamic-update-slice(f32[8,257,128]{2,0,1:T(8,128)} %get-tuple-element.162, f32[1,257,128]{2,0,1:T(1,128)S(1)} %copy.59, s32[]{:T(128)} %get-tuple-element.161, s32[]{:T(128)} %constant.54.clone.1..sunk, s32[]{:T(128)} %constant.54.clone.1..sunk) | dynamic-update-slice | bytes 263172 | tf_op jit(solution)/shard_map/while/body/jit(dynamic_update_index_in_dim)/dynamic_update_slice | solution.py:100
  138.9 4.0 rev.8
  143.5 5.0 %dynamic_update_slice.9 = f32[8,257,128]{2,0,1:T(8,128)} dynamic-update-slice(f32[8,257,128]{2,0,1:T(8,128)} %get-tuple-element.162, f32[1,257,128]{2,0,1:T(1,128)S(1)} %copy.59, s32[]{:T(128)} %get-tuple-element.161, s32[]{:T(128)} %constant.54.clone.1..sunk, s32[]{:T(128)} %constant.54.clone.1..sunk) | dynamic-update-slice | bytes 263172 | tf_op jit(solution)/shard_map/while/body/jit(dynamic_update_index_in_dim)/dynamic_update_slice | solution.py:100
  152.4 4.0 rev.8
  157.0 5.0 %dynamic_update_slice.9 = f32[8,257,128]{2,0,1:T(8,128)} dynamic-update-slice(f32[8,257,128]{2,0,1:T(8,128)} %get-tuple-element.162, f32[1,257,128]{2,0,1:T(1,128)S(1)} %copy.59, s32[]{:T(128)} %get-tuple-element.161, s32[]{:T(128)} %constant.54.clone.1..sunk, s32[]{:T(128)} %constant.54.clone.1..sunk) | dynamic-update-slice | bytes 263172 | tf_op jit(solution)/shard_map/while/body/jit(dynamic_update_index_in_dim)/dynamic_update_slice | solution.py:100
  165.9 4.0 rev.8
  170.5 5.0 %dynamic_update_slice.9 = f32[8,257,128]{2,0,1:T(8,128)} dynamic-update-slice(f32[8,257,128]{2,0,1:T(8,128)} %get-tuple-element.162, f32[1,257,128]{2,0,1:T(1,128)S(1)} %copy.59, s32[]{:T(128)} %get-tuple-element.161, s32[]{:T(128)} %constant.54.clone.1..sunk, s32[]{:T(128)} %constant.54.clone.1..sunk) | dynamic-update-slice | bytes 263172 | tf_op jit(solution)/shard_map/while/body/jit(dynamic_update_index_in_dim)/dynamic_update_slice | solution.py:100
  179.3 4.0 rev.8
  184.0 5.0 %dynamic_update_slice.9 = f32[8,257,128]{2,0,1:T(8,128)} dynamic-update-slice(f32[8,257,128]{2,0,1:T(8,128)} %get-tuple-element.162, f32[1,257,128]{2,0,1:T(1,128)S(1)} %copy.59, s32[]{:T(128)} %get-tuple-element.161, s32[]{:T(128)} %constant.54.clone.1..sunk, s32[]{:T(128)} %constant.54.clone.1..sunk) | dynamic-update-slice | bytes 263172 | tf_op jit(solution)/shard_map/while/body/jit(dynamic_update_index_in_dim)/dynamic_update_slice | solution.py:100
  192.8 4.0 rev.8
  197.4 5.0 %dynamic_update_slice.9 = f32[8,257,128]{2,0,1:T(8,128)} dynamic-update-slice(f32[8,257,128]{2,0,1:T(8,128)} %get-tuple-element.162, f32[1,257,128]{2,0,1:T(1,128)S(1)} %copy.59, s32[]{:T(128)} %get-tuple-element.161, s32[]{:T(128)} %constant.54.clone.1..sunk, s32[]{:T(128)} %constant.54.clone.1..sunk) | dynamic-update-slice | bytes 263172 | tf_op jit(solution)/shard_map/while/body/jit(dynamic_update_index_in_dim)/dynamic_update_slice | solution.py:100
  206.3 4.0 rev.8
  210.9 5.0 %dynamic_update_slice.9 = f32[8,257,128]{2,0,1:T(8,128)} dynamic-update-slice(f32[8,257,128]{2,0,1:T(8,128)} %get-tuple-element.162, f32[1,257,128]{2,0,1:T(1,128)S(1)} %copy.59, s32[]{:T(128)} %get-tuple-element.161, s32[]{:T(128)} %constant.54.clone.1..sunk, s32[]{:T(128)} %constant.54.clone.1..sunk) | dynamic-update-slice | bytes 263172 | tf_op jit(solution)/shard_map/while/body/jit(dynamic_update_index_in_dim)/dynamic_update_slice | solution.py:100
  217.0 108.1 %while.21 = (s32[]{:T(128)}, f32[8,257,128]{2,0,1:T(8,128)}, bf16[8,2304]{1,0:T(8,128)(2,1)S(1)}, bf16[128,2048]{1,0:T(8,128)(2,1)S(1)}, s32[]{:T(128)}, /*index=5*/s32[]{:T(128)}) while((s32[]{:T(128)}, f32[8,257,128]{2,0,1:T(8,128)}, bf16[8,2304]{1,0:T(8,128)(2,1)S(1)}, bf16[128,2048]{1,0:T(8,128)(2,1)S(1)}, s32[]{:T(128)}, ...), condition=%wide.region_6.7_spmd, body=%wide.region_5.6_spmd.sunk | while | flops 134742016 | bytes 14765141 | solution.py:100
  220.8 4.0 rev.9
  225.4 5.0 %dynamic_update_slice.10 = f32[8,257,128]{2,0,1:T(8,128)} dynamic-update-slice(f32[8,257,128]{2,0,1:T(8,128)} %get-tuple-element.144, f32[1,257,128]{2,0,1:T(1,128)S(1)} %copy.60, s32[]{:T(128)} %get-tuple-element.143, s32[]{:T(128)} %constant.54.clone.1..sunk.1, s32[]{:T(128)} %constant.54.clone.1..sunk.1) | dynamic-update-slice | bytes 263172 | tf_op jit(solution)/shard_map/while/body/jit(dynamic_update_index_in_dim)/dynamic_update_slice | solution.py:100
  234.3 4.0 rev.9
  238.9 5.0 %dynamic_update_slice.10 = f32[8,257,128]{2,0,1:T(8,128)} dynamic-update-slice(f32[8,257,128]{2,0,1:T(8,128)} %get-tuple-element.144, f32[1,257,128]{2,0,1:T(1,128)S(1)} %copy.60, s32[]{:T(128)} %get-tuple-element.143, s32[]{:T(128)} %constant.54.clone.1..sunk.1, s32[]{:T(128)} %constant.54.clone.1..sunk.1) | dynamic-update-slice | bytes 263172 | tf_op jit(solution)/shard_map/while/body/jit(dynamic_update_index_in_dim)/dynamic_update_slice | solution.py:100
  252.5 5.0 %dynamic_update_slice.10 = f32[8,257,128]{2,0,1:T(8,128)} dynamic-update-slice(f32[8,257,128]{2,0,1:T(8,128)} %get-tuple-element.144, f32[1,257,128]{2,0,1:T(1,128)S(1)} %copy.60, s32[]{:T(128)} %get-tuple-element.143, s32[]{:T(128)} %constant.54.clone.1..sunk.1, s32[]{:T(128)} %constant.54.clone.1..sunk.1) | dynamic-update-slice | bytes 263172 | tf_op jit(solution)/shard_map/while/body/jit(dynamic_update_index_in_dim)/dynamic_update_slice | solution.py:100
  266.0 5.0 %dynamic_update_slice.10 = f32[8,257,128]{2,0,1:T(8,128)} dynamic-update-slice(f32[8,257,128]{2,0,1:T(8,128)} %get-tuple-element.144, f32[1,257,128]{2,0,1:T(1,128)S(1)} %copy.60, s32[]{:T(128)} %get-tuple-element.143, s32[]{:T(128)} %constant.54.clone.1..sunk.1, s32[]{:T(128)} %constant.54.clone.1..sunk.1) | dynamic-update-slice | bytes 263172 | tf_op jit(solution)/shard_map/while/body/jit(dynamic_update_index_in_dim)/dynamic_update_slice | solution.py:100
  279.5 5.0 %dynamic_update_slice.10 = f32[8,257,128]{2,0,1:T(8,128)} dynamic-update-slice(f32[8,257,128]{2,0,1:T(8,128)} %get-tuple-element.144, f32[1,257,128]{2,0,1:T(1,128)S(1)} %copy.60, s32[]{:T(128)} %get-tuple-element.143, s32[]{:T(128)} %constant.54.clone.1..sunk.1, s32[]{:T(128)} %constant.54.clone.1..sunk.1) | dynamic-update-slice | bytes 263172 | tf_op jit(solution)/shard_map/while/body/jit(dynamic_update_index_in_dim)/dynamic_update_slice | solution.py:100
  293.0 5.0 %dynamic_update_slice.10 = f32[8,257,128]{2,0,1:T(8,128)} dynamic-update-slice(f32[8,257,128]{2,0,1:T(8,128)} %get-tuple-element.144, f32[1,257,128]{2,0,1:T(1,128)S(1)} %copy.60, s32[]{:T(128)} %get-tuple-element.143, s32[]{:T(128)} %constant.54.clone.1..sunk.1, s32[]{:T(128)} %constant.54.clone.1..sunk.1) | dynamic-update-slice | bytes 263172 | tf_op jit(solution)/shard_map/while/body/jit(dynamic_update_index_in_dim)/dynamic_update_slice | solution.py:100
  306.5 5.0 %dynamic_update_slice.10 = f32[8,257,128]{2,0,1:T(8,128)} dynamic-update-slice(f32[8,257,128]{2,0,1:T(8,128)} %get-tuple-element.144, f32[1,257,128]{2,0,1:T(1,128)S(1)} %copy.60, s32[]{:T(128)} %get-tuple-element.143, s32[]{:T(128)} %constant.54.clone.1..sunk.1, s32[]{:T(128)} %constant.54.clone.1..sunk.1) | dynamic-update-slice | bytes 263172 | tf_op jit(solution)/shard_map/while/body/jit(dynamic_update_index_in_dim)/dynamic_update_slice | solution.py:100
  320.0 5.0 %dynamic_update_slice.10 = f32[8,257,128]{2,0,1:T(8,128)} dynamic-update-slice(f32[8,257,128]{2,0,1:T(8,128)} %get-tuple-element.144, f32[1,257,128]{2,0,1:T(1,128)S(1)} %copy.60, s32[]{:T(128)} %get-tuple-element.143, s32[]{:T(128)} %constant.54.clone.1..sunk.1, s32[]{:T(128)} %constant.54.clone.1..sunk.1) | dynamic-update-slice | bytes 263172 | tf_op jit(solution)/shard_map/while/body/jit(dynamic_update_index_in_dim)/dynamic_update_slice | solution.py:100
  330.1 59.8 %all-reduce.7.cloned.1.call-done = f32[2,8,257,128]{3,1,2,0:T(8,128)} async-done(((f32[2,8,257,128]{3,1,2,0:T(8,128)}), f32[2,8,257,128]{3,1,2,0:T(8,128)}) %all-reduce.7.cloned.1.call-update) | async-done | bytes 2105360
  (190 shorter events, 131.0 us)
Async XLA Ops:
  6.5 8.2 %copy-start.1 = (bf16[64]{0:T(256)(128)(2,1)S(1)}, bf16[64]{0:T(256)(128)(2,1)}, u32[]{:S(2)}) copy-start(bf16[64]{0:T(256)(128)(2,1)} %param.8) | copy-start | bytes 388
  6.5 8.3 %copy-start = (s32[2,8]{1,0:T(2,128)S(1)}, s32[2,8]{1,0:T(2,128)}, u32[]{:S(2)}) copy-start(s32[2,8]{1,0:T(2,128)} %param.9) | copy-start | bytes 196
  6.5 383.4 %all-reduce.7.cloned.1.call-start = ((), (), s32[]{:S(2)}) async-start(), calls=%async_computation | async-start | bytes 4210688
  9.8 12.0 %collective-permute-start = (bf16[128,64]{0,1:T(8,128)(2,1)S(1)}, bf16[128,64]{0,1:T(8,128)(2,1)S(1)}, u32[]{:S(2)}, u32[]{:S(2)}) collective-permute-start(bf16[128,64]{0,1:T(8,128)(2,1)S(1)} %slice.86), channel_id=1, source_target_pairs={{0,1},{2,3},{4,5},{6,7},{8,9},{10,11},{12,13},{14,15},{16,17},{18,... | collective-permute-start | bytes 49160 | tf_op jit(solution)/shard_map/ppermute | solution.py:19
  25.6 3.0 collective-permute-start.1
  26.9 5.6 %collective-permute-start.2 = (f32[128,32]{0,1:T(8,128)S(1)}, f32[128,32]{0,1:T(8,128)S(1)}, u32[]{:S(2)}, u32[]{:S(2)}) collective-permute-start(f32[128,32]{0,1:T(8,128)S(1)} %get-tuple-element.74), channel_id=1, source_target_pairs={{1,0},{3,2},{5,4},{7,6},{9,8},{11,10},{13,12},{15,14},{17,16},{19,... | collective-permute-start | bytes 49160 | tf_op jit(solution)/shard_map/ppermute | solution.py:30
  97.8 9.3 %collective-permute-start.3 = (bf16[8,128]{1,0:T(8,128)(2,1)S(1)}, bf16[8,128]{1,0:T(8,128)(2,1)S(1)}, u32[]{:S(2)}, u32[]{:S(2)}) collective-permute-start(bf16[8,128]{1,0:T(8,128)(2,1)S(1)} %get-tuple-element.75), channel_id=1, source_target_pairs={{0,1},{2,3},{4,5},{6,7},{8,9},{10,11},{12,13},{14,15},{16,17},{18,... | collective-permute-start | bytes 6152 | tf_op jit(solution)/shard_map/ppermute | solution.py:29
  99.7 7.4 %collective-permute-start.4 = (bf16[8,128]{1,0:T(8,128)(2,1)S(1)}, bf16[8,128]{1,0:T(8,128)(2,1)S(1)}, u32[]{:S(2)}, u32[]{:S(2)}) collective-permute-start(bf16[8,128]{1,0:T(8,128)(2,1)S(1)} %get-tuple-element.76), channel_id=1, source_target_pairs={{1,0},{3,2},{5,4},{7,6},{9,8},{11,10},{13,12},{15,14},{17,16},{19,... | collective-permute-start | bytes 6152 | tf_op jit(solution)/shard_map/ppermute | solution.py:30
  101.0 114.9 %collective-permute-start.5 = (bf16[8,128]{1,0:T(8,128)(2,1)S(1)}, bf16[8,128]{1,0:T(8,128)(2,1)S(1)}, u32[]{:S(2)}, u32[]{:S(2)}) collective-permute-start(bf16[8,128]{1,0:T(8,128)(2,1)S(1)} %get-tuple-element.77), channel_id=1, source_target_pairs={{0,1},{2,3},{4,5},{6,7},{8,9},{10,11},{12,13},{14,15},{16,17},{18,... | collective-permute-start | bytes 6152 | tf_op jit(solution)/shard_map/ppermute | solution.py:29
  105.6 110.4 %collective-permute-start.6 = (bf16[8,128]{1,0:T(8,128)(2,1)S(1)}, bf16[8,128]{1,0:T(8,128)(2,1)S(1)}, u32[]{:S(2)}, u32[]{:S(2)}) collective-permute-start(bf16[8,128]{1,0:T(8,128)(2,1)S(1)} %get-tuple-element.78), channel_id=1, source_target_pairs={{1,0},{3,2},{5,4},{7,6},{9,8},{11,10},{13,12},{15,14},{17,16},{19,... | collective-permute-start | bytes 6152 | tf_op jit(solution)/shard_map/ppermute | solution.py:30
  328.2 0.7 copy-start.2
Sparse Core Ops, SparseCore 0:
  328.4 61.4 all-reduce.6
where the time goes:
time: 402 us; the launch traced here: 399 us
  local copies, waits for them, and re-layouts  221 us (55%)
  waiting for transfers between devices  63.8 us (16%)
  blocking collectives  60.9 us (15%)
  starting transfers between devices  16.7 us (4%)
  between operations  14.4 us (4%)
  other arithmetic  11.8 us (3%)
  matrix products  9.57 us (2%)
    dynamic_update_slice x32, local copies, waits for them, and re-layouts, lag_products(): return lax.map(single, extended_traces)  82.6 us
    rev x16, local copies, waits for them, and re-layouts, single(): toeplitz = tiled[::-1, :length]  63.6 us
    psum x1, blocking collectives, per_device(): lax.psum(jnp.dot(picks.astype(jnp.bfloat16), white, preferred_element_typ...  60.9 us
    unnamed x2, waiting for transfers between devices  59.8 us
    reshape x16, local copies, waits for them, and re-layouts, single(): jnp.tile(trace, LAGS + 1)[:LAGS * (width + 1)].reshape(LAGS, width + 1)  33.7 us
    another operation x32, local copies, waits for them, and re-layouts, single(): jnp.tile(trace, LAGS + 1)[:LAGS * (width + 1)].reshape(LAGS, width + 1)  23.4 us
  transfers between devices with their start and end apart: 8, of which 2 were waited for; matrix products, arithmetic and copies ran while one was open for 29% of the time, Pallas kernels for 0%

commit v1 on v0

--- a/solution.py
+++ b/solution.py
@@ -117,9 +117,9 @@
         picks = (local_rows[step_index][:, None] == jnp.arange(channel_count)[None, :]) & (
             owner_ids[step_index][:, None] == my_block
         )
-        summed = lax.psum(
-            jnp.dot(picks.astype(jnp.bfloat16), white, preferred_element_type=jnp.float32), "chan"
-        )
+        own_rows = jnp.dot(picks.astype(jnp.bfloat16), white, preferred_element_type=jnp.float32)
+        known = lax.all_gather(own_rows, "chan")
+        summed = jnp.sum(known, axis=0)
         traces.append(summed.astype(jnp.bfloat16))
     scale = 1.0 / math.sqrt(dec_dev * lax.axis_size("tm"))
     terms = []

time: 402 us -> 417 us (1.037)
  waiting for transfers between devices: 63.8 us -> 136 us
  blocking collectives: 60.9 us -> 0 us
    all_gather x0 -> x2, waiting for transfers between devices: none -> 70.5 us  [per_device(): known = lax.all_gather(own_rows, 'chan')]
    psum x1 -> x0, blocking collectives: 60.9 us -> none  [per_device(): lax.psum(jnp.dot(picks.astype(jnp.bfloat16), white, preferred_element_typ...]
    unnamed x2 -> x4, waiting for transfers between devices: 59.8 us -> 61.5 us
  transfers between devices with their start and end apart: 8 -> 10, of which waited for: 2 -> 4; matrix products, arithmetic and copies ran while one was open for 29% -> 29% of each run, Pallas kernels for 0% -> 0%
where the time goes in v1:
time: 417 us; the launch traced here: 415 us
  local copies, waits for them, and re-layouts  221 us (53%)
  waiting for transfers between devices  136 us (33%)
  starting transfers between devices  17.1 us (4%)
  other arithmetic  14.4 us (3%)
  between operations  14.1 us (3%)
  matrix products  10.8 us (3%)
    dynamic_update_slice x32, local copies, waits for them, and re-layouts, lag_products(): return lax.map(single, extended_traces)  82.6 us
    all_gather x2, waiting for transfers between devices, per_device(): known = lax.all_gather(own_rows, 'chan')  70.5 us
    rev x16, local copies, waits for them, and re-layouts, single(): toeplitz = tiled[::-1, :length]  63.6 us
    unnamed x4, waiting for transfers between devices  61.5 us
    reshape x16, local copies, waits for them, and re-layouts, single(): jnp.tile(trace, LAGS + 1)[:LAGS * (width + 1)].reshape(LAGS, width + 1)  33.7 us
    another operation x32, local copies, waits for them, and re-layouts, single(): jnp.tile(trace, LAGS + 1)[:LAGS * (width + 1)].reshape(LAGS, width + 1)  23.4 us
  transfers between devices with their start and end apart: 10, of which 4 were waited for; matrix products, arithmetic and copies ran while one was open for 29% of the time, Pallas kernels for 0%

profile of v1, /device:TPU:0, one launch (start us, length us, event | category | flops | bytes accessed | tf_op | source)
XLA Modules:
  0.0 414.6 jit_solution(8137210842604876744)
XLA Ops:
  9.8 4.9 %collective-permute-start = (bf16[128,64]{0,1:T(8,128)(2,1)S(1)}, bf16[128,64]{0,1:T(8,128)(2,1)S(1)}, u32[]{:S(2)}, u32[]{:S(2)}) collective-permute-start(bf16[128,64]{0,1:T(8,128)(2,1)S(1)} %slice.86), channel_id=1, source_target_pairs={{0,1},{2,3},{4,5},{6,7},{8,9},{10,11},{12,13},{14,15},{16,17},{18,... | collective-permute-start | bytes 49160 | tf_op jit(solution)/shard_map/ppermute | solution.py:19
  14.8 6.9 %select_reduce_fusion = bf16[144,4,128]{2,1,0:T(4,128)(2,1)S(1)} fusion(f32[64]{0:T(128)S(1)} %convert_element_type.22, s32[144,4,128]{2,1,0:T(4,128)S(1)} %iota_subtract_fusion), kind=kLoop, calls=%fused_computation.4 | loop fusion | flops 14082048 | bytes 442624 | tf_op jit(solution)/shard_map/reduce_sum | solution.py:42
  38.3 37.4 %all-gather.5.cloned.1.call-done = f32[128,2048]{1,0:T(8,128)} async-done(((f32[8,2048]{1,0:T(8,128)}), f32[128,2048]{1,0:T(8,128)}) %all-gather.5.cloned.1.call-update) | async-done | bytes 1048592 | tf_op jit(solution)/shard_map/all_gather | solution.py:121
  81.6 33.1 %all-gather.7.cloned.1.call-done = f32[128,2048]{1,0:T(8,128)} async-done(((f32[8,2048]{1,0:T(8,128)}), f32[128,2048]{1,0:T(8,128)}) %all-gather.7.cloned.1.call-update) | async-done | bytes 1048592 | tf_op jit(solution)/shard_map/all_gather | solution.py:121
  122.0 107.7 %while.20 = (s32[]{:T(128)}, f32[8,257,128]{2,0,1:T(8,128)}, bf16[8,2304]{1,0:T(8,128)(2,1)S(1)}, bf16[128,2048]{1,0:T(8,128)(2,1)S(1)}, s32[]{:T(128)}, /*index=5*/s32[]{:T(128)}) while((s32[]{:T(128)}, f32[8,257,128]{2,0,1:T(8,128)}, bf16[8,2304]{1,0:T(8,128)(2,1)S(1)}, bf16[128,2048]{1,0:T(8,128)(2,1)S(1)}, s32[]{:T(128)}, ...), condition=%wide.region_3.4_spmd, body=%wide.region_2.3_spmd.sunk | while | flops 134742016 | bytes 14765141 | solution.py:100
  125.8 4.0 rev.8
  130.4 5.0 %dynamic_update_slice.9 = f32[8,257,128]{2,0,1:T(8,128)} dynamic-update-slice(f32[8,257,128]{2,0,1:T(8,128)} %get-tuple-element.160, f32[1,257,128]{2,0,1:T(1,128)S(1)} %copy.61, s32[]{:T(128)} %get-tuple-element.159, s32[]{:T(128)} %constant.54.clone.1..sunk, s32[]{:T(128)} %constant.54.clone.1..sunk) | dynamic-update-slice | bytes 263172 | tf_op jit(solution)/shard_map/while/body/jit(dynamic_update_index_in_dim)/dynamic_update_slice | solution.py:100
  139.3 4.0 rev.8
  143.9 5.0 %dynamic_update_slice.9 = f32[8,257,128]{2,0,1:T(8,128)} dynamic-update-slice(f32[8,257,128]{2,0,1:T(8,128)} %get-tuple-element.160, f32[1,257,128]{2,0,1:T(1,128)S(1)} %copy.61, s32[]{:T(128)} %get-tuple-element.159, s32[]{:T(128)} %constant.54.clone.1..sunk, s32[]{:T(128)} %constant.54.clone.1..sunk) | dynamic-update-slice | bytes 263172 | tf_op jit(solution)/shard_map/while/body/jit(dynamic_update_index_in_dim)/dynamic_update_slice | solution.py:100
  152.7 4.0 rev.8
  157.4 5.0 %dynamic_update_slice.9 = f32[8,257,128]{2,0,1:T(8,128)} dynamic-update-slice(f32[8,257,128]{2,0,1:T(8,128)} %get-tuple-element.160, f32[1,257,128]{2,0,1:T(1,128)S(1)} %copy.61, s32[]{:T(128)} %get-tuple-element.159, s32[]{:T(128)} %constant.54.clone.1..sunk, s32[]{:T(128)} %constant.54.clone.1..sunk) | dynamic-update-slice | bytes 263172 | tf_op jit(solution)/shard_map/while/body/jit(dynamic_update_index_in_dim)/dynamic_update_slice | solution.py:100
  166.2 4.0 rev.8
  170.8 5.0 %dynamic_update_slice.9 = f32[8,257,128]{2,0,1:T(8,128)} dynamic-update-slice(f32[8,257,128]{2,0,1:T(8,128)} %get-tuple-element.160, f32[1,257,128]{2,0,1:T(1,128)S(1)} %copy.61, s32[]{:T(128)} %get-tuple-element.159, s32[]{:T(128)} %constant.54.clone.1..sunk, s32[]{:T(128)} %constant.54.clone.1..sunk) | dynamic-update-slice | bytes 263172 | tf_op jit(solution)/shard_map/while/body/jit(dynamic_update_index_in_dim)/dynamic_update_slice | solution.py:100
  184.3 5.0 %dynamic_update_slice.9 = f32[8,257,128]{2,0,1:T(8,128)} dynamic-update-slice(f32[8,257,128]{2,0,1:T(8,128)} %get-tuple-element.160, f32[1,257,128]{2,0,1:T(1,128)S(1)} %copy.61, s32[]{:T(128)} %get-tuple-element.159, s32[]{:T(128)} %constant.54.clone.1..sunk, s32[]{:T(128)} %constant.54.clone.1..sunk) | dynamic-update-slice | bytes 263172 | tf_op jit(solution)/shard_map/while/body/jit(dynamic_update_index_in_dim)/dynamic_update_slice | solution.py:100
  193.1 4.0 rev.8
  197.7 5.0 %dynamic_update_slice.9 = f32[8,257,128]{2,0,1:T(8,128)} dynamic-update-slice(f32[8,257,128]{2,0,1:T(8,128)} %get-tuple-element.160, f32[1,257,128]{2,0,1:T(1,128)S(1)} %copy.61, s32[]{:T(128)} %get-tuple-element.159, s32[]{:T(128)} %constant.54.clone.1..sunk, s32[]{:T(128)} %constant.54.clone.1..sunk) | dynamic-update-slice | bytes 263172 | tf_op jit(solution)/shard_map/while/body/jit(dynamic_update_index_in_dim)/dynamic_update_slice | solution.py:100
  206.6 4.0 rev.8
  211.2 5.0 %dynamic_update_slice.9 = f32[8,257,128]{2,0,1:T(8,128)} dynamic-update-slice(f32[8,257,128]{2,0,1:T(8,128)} %get-tuple-element.160, f32[1,257,128]{2,0,1:T(1,128)S(1)} %copy.61, s32[]{:T(128)} %get-tuple-element.159, s32[]{:T(128)} %constant.54.clone.1..sunk, s32[]{:T(128)} %constant.54.clone.1..sunk) | dynamic-update-slice | bytes 263172 | tf_op jit(solution)/shard_map/while/body/jit(dynamic_update_index_in_dim)/dynamic_update_slice | solution.py:100
  220.1 4.0 rev.8
  224.7 5.0 %dynamic_update_slice.9 = f32[8,257,128]{2,0,1:T(8,128)} dynamic-update-slice(f32[8,257,128]{2,0,1:T(8,128)} %get-tuple-element.160, f32[1,257,128]{2,0,1:T(1,128)S(1)} %copy.61, s32[]{:T(128)} %get-tuple-element.159, s32[]{:T(128)} %constant.54.clone.1..sunk, s32[]{:T(128)} %constant.54.clone.1..sunk) | dynamic-update-slice | bytes 263172 | tf_op jit(solution)/shard_map/while/body/jit(dynamic_update_index_in_dim)/dynamic_update_slice | solution.py:100
  230.7 108.1 %while.21 = (s32[]{:T(128)}, f32[8,257,128]{2,0,1:T(8,128)}, bf16[8,2304]{1,0:T(8,128)(2,1)S(1)}, bf16[128,2048]{1,0:T(8,128)(2,1)S(1)}, s32[]{:T(128)}, /*index=5*/s32[]{:T(128)}) while((s32[]{:T(128)}, f32[8,257,128]{2,0,1:T(8,128)}, bf16[8,2304]{1,0:T(8,128)(2,1)S(1)}, bf16[128,2048]{1,0:T(8,128)(2,1)S(1)}, s32[]{:T(128)}, ...), condition=%wide.region_6.7_spmd, body=%wide.region_5.6_spmd.sunk | while | flops 134742016 | bytes 14765141 | solution.py:100
  234.6 4.0 rev.9
  239.2 5.0 %dynamic_update_slice.10 = f32[8,257,128]{2,0,1:T(8,128)} dynamic-update-slice(f32[8,257,128]{2,0,1:T(8,128)} %get-tuple-element.142, f32[1,257,128]{2,0,1:T(1,128)S(1)} %copy.62, s32[]{:T(128)} %get-tuple-element.141, s32[]{:T(128)} %constant.54.clone.1..sunk.1, s32[]{:T(128)} %constant.54.clone.1..sunk.1) | dynamic-update-slice | bytes 263172 | tf_op jit(solution)/shard_map/while/body/jit(dynamic_update_index_in_dim)/dynamic_update_slice | solution.py:100
  248.1 4.0 rev.9
  252.7 5.0 %dynamic_update_slice.10 = f32[8,257,128]{2,0,1:T(8,128)} dynamic-update-slice(f32[8,257,128]{2,0,1:T(8,128)} %get-tuple-element.142, f32[1,257,128]{2,0,1:T(1,128)S(1)} %copy.62, s32[]{:T(128)} %get-tuple-element.141, s32[]{:T(128)} %constant.54.clone.1..sunk.1, s32[]{:T(128)} %constant.54.clone.1..sunk.1) | dynamic-update-slice | bytes 263172 | tf_op jit(solution)/shard_map/while/body/jit(dynamic_update_index_in_dim)/dynamic_update_slice | solution.py:100
  266.2 5.0 %dynamic_update_slice.10 = f32[8,257,128]{2,0,1:T(8,128)} dynamic-update-slice(f32[8,257,128]{2,0,1:T(8,128)} %get-tuple-element.142, f32[1,257,128]{2,0,1:T(1,128)S(1)} %copy.62, s32[]{:T(128)} %get-tuple-element.141, s32[]{:T(128)} %constant.54.clone.1..sunk.1, s32[]{:T(128)} %constant.54.clone.1..sunk.1) | dynamic-update-slice | bytes 263172 | tf_op jit(solution)/shard_map/while/body/jit(dynamic_update_index_in_dim)/dynamic_update_slice | solution.py:100
  279.7 5.0 %dynamic_update_slice.10 = f32[8,257,128]{2,0,1:T(8,128)} dynamic-update-slice(f32[8,257,128]{2,0,1:T(8,128)} %get-tuple-element.142, f32[1,257,128]{2,0,1:T(1,128)S(1)} %copy.62, s32[]{:T(128)} %get-tuple-element.141, s32[]{:T(128)} %constant.54.clone.1..sunk.1, s32[]{:T(128)} %constant.54.clone.1..sunk.1) | dynamic-update-slice | bytes 263172 | tf_op jit(solution)/shard_map/while/body/jit(dynamic_update_index_in_dim)/dynamic_update_slice | solution.py:100
  293.3 5.0 %dynamic_update_slice.10 = f32[8,257,128]{2,0,1:T(8,128)} dynamic-update-slice(f32[8,257,128]{2,0,1:T(8,128)} %get-tuple-element.142, f32[1,257,128]{2,0,1:T(1,128)S(1)} %copy.62, s32[]{:T(128)} %get-tuple-element.141, s32[]{:T(128)} %constant.54.clone.1..sunk.1, s32[]{:T(128)} %constant.54.clone.1..sunk.1) | dynamic-update-slice | bytes 263172 | tf_op jit(solution)/shard_map/while/body/jit(dynamic_update_index_in_dim)/dynamic_update_slice | solution.py:100
  306.8 5.0 %dynamic_update_slice.10 = f32[8,257,128]{2,0,1:T(8,128)} dynamic-update-slice(f32[8,257,128]{2,0,1:T(8,128)} %get-tuple-element.142, f32[1,257,128]{2,0,1:T(1,128)S(1)} %copy.62, s32[]{:T(128)} %get-tuple-element.141, s32[]{:T(128)} %constant.54.clone.1..sunk.1, s32[]{:T(128)} %constant.54.clone.1..sunk.1) | dynamic-update-slice | bytes 263172 | tf_op jit(solution)/shard_map/while/body/jit(dynamic_update_index_in_dim)/dynamic_update_slice | solution.py:100
  320.3 5.0 %dynamic_update_slice.10 = f32[8,257,128]{2,0,1:T(8,128)} dynamic-update-slice(f32[8,257,128]{2,0,1:T(8,128)} %get-tuple-element.142, f32[1,257,128]{2,0,1:T(1,128)S(1)} %copy.62, s32[]{:T(128)} %get-tuple-element.141, s32[]{:T(128)} %constant.54.clone.1..sunk.1, s32[]{:T(128)} %constant.54.clone.1..sunk.1) | dynamic-update-slice | bytes 263172 | tf_op jit(solution)/shard_map/while/body/jit(dynamic_update_index_in_dim)/dynamic_update_slice | solution.py:100
  333.8 5.0 %dynamic_update_slice.10 = f32[8,257,128]{2,0,1:T(8,128)} dynamic-update-slice(f32[8,257,128]{2,0,1:T(8,128)} %get-tuple-element.142, f32[1,257,128]{2,0,1:T(1,128)S(1)} %copy.62, s32[]{:T(128)} %get-tuple-element.141, s32[]{:T(128)} %constant.54.clone.1..sunk.1, s32[]{:T(128)} %constant.54.clone.1..sunk.1) | dynamic-update-slice | bytes 263172 | tf_op jit(solution)/shard_map/while/body/jit(dynamic_update_index_in_dim)/dynamic_update_slice | solution.py:100
  343.9 61.5 %all-reduce.5.cloned.1.call-done = f32[2,8,257,128]{3,1,2,0:T(8,128)} async-done(((f32[2,8,257,128]{3,1,2,0:T(8,128)}), f32[2,8,257,128]{3,1,2,0:T(8,128)}) %all-reduce.5.cloned.1.call-update) | async-done | bytes 2105360
  (197 shorter events, 139.7 us)
Async XLA Ops:
  6.5 8.2 %copy-start.1 = (bf16[64]{0:T(256)(128)(2,1)S(1)}, bf16[64]{0:T(256)(128)(2,1)}, u32[]{:S(2)}) copy-start(bf16[64]{0:T(256)(128)(2,1)} %param.8) | copy-start | bytes 388
  6.5 8.3 %copy-start = (s32[2,8]{1,0:T(2,128)S(1)}, s32[2,8]{1,0:T(2,128)}, u32[]{:S(2)}) copy-start(s32[2,8]{1,0:T(2,128)} %param.9) | copy-start | bytes 196
  6.5 69.1 %all-gather.5.cloned.1.call-start = ((), (), s32[]{:S(2)}) async-start(), calls=%async_computation | async-start | bytes 1114112 | tf_op jit(solution)/shard_map/all_gather | solution.py:121
  9.8 12.0 %collective-permute-start = (bf16[128,64]{0,1:T(8,128)(2,1)S(1)}, bf16[128,64]{0,1:T(8,128)(2,1)S(1)}, u32[]{:S(2)}, u32[]{:S(2)}) collective-permute-start(bf16[128,64]{0,1:T(8,128)(2,1)S(1)} %slice.86), channel_id=1, source_target_pairs={{0,1},{2,3},{4,5},{6,7},{8,9},{10,11},{12,13},{14,15},{16,17},{18,... | collective-permute-start | bytes 49160 | tf_op jit(solution)/shard_map/ppermute | solution.py:19
  25.6 3.0 collective-permute-start.1
  26.9 5.6 %collective-permute-start.2 = (f32[128,32]{0,1:T(8,128)S(1)}, f32[128,32]{0,1:T(8,128)S(1)}, u32[]{:S(2)}, u32[]{:S(2)}) collective-permute-start(f32[128,32]{0,1:T(8,128)S(1)} %get-tuple-element.72), channel_id=1, source_target_pairs={{1,0},{3,2},{5,4},{7,6},{9,8},{11,10},{13,12},{15,14},{17,16},{19,... | collective-permute-start | bytes 49160 | tf_op jit(solution)/shard_map/ppermute | solution.py:30
  37.3 77.4 %all-gather.7.cloned.1.call-start = ((), (), s32[]{:S(2)}) async-start(), calls=%async_computation.1 | async-start | bytes 1114112 | tf_op jit(solution)/shard_map/all_gather | solution.py:121
  38.2 367.1 %all-reduce.5.cloned.1.call-start = ((), (), s32[]{:S(2)}) async-start(), calls=%async_computation.2 | async-start | bytes 4210688
  77.0 43.9 %collective-permute-start.3 = (bf16[8,128]{1,0:T(8,128)(2,1)S(1)}, bf16[8,128]{1,0:T(8,128)(2,1)S(1)}, u32[]{:S(2)}, u32[]{:S(2)}) collective-permute-start(bf16[8,128]{1,0:T(8,128)(2,1)S(1)} %get-tuple-element.73), channel_id=1, source_target_pairs={{0,1},{2,3},{4,5},{6,7},{8,9},{10,11},{12,13},{14,15},{16,17},{18,... | collective-permute-start | bytes 6152 | tf_op jit(solution)/shard_map/ppermute | solution.py:29
  80.3 40.5 %collective-permute-start.4 = (bf16[8,128]{1,0:T(8,128)(2,1)S(1)}, bf16[8,128]{1,0:T(8,128)(2,1)S(1)}, u32[]{:S(2)}, u32[]{:S(2)}) collective-permute-start(bf16[8,128]{1,0:T(8,128)(2,1)S(1)} %get-tuple-element.74), channel_id=1, source_target_pairs={{1,0},{3,2},{5,4},{7,6},{9,8},{11,10},{13,12},{15,14},{17,16},{19,... | collective-permute-start | bytes 6152 | tf_op jit(solution)/shard_map/ppermute | solution.py:30
  116.0 113.7 %collective-permute-start.5 = (bf16[8,128]{1,0:T(8,128)(2,1)S(1)}, bf16[8,128]{1,0:T(8,128)(2,1)S(1)}, u32[]{:S(2)}, u32[]{:S(2)}) collective-permute-start(bf16[8,128]{1,0:T(8,128)(2,1)S(1)} %get-tuple-element.75), channel_id=1, source_target_pairs={{0,1},{2,3},{4,5},{6,7},{8,9},{10,11},{12,13},{14,15},{16,17},{18,... | collective-permute-start | bytes 6152 | tf_op jit(solution)/shard_map/ppermute | solution.py:29
  119.4 110.3 %collective-permute-start.6 = (bf16[8,128]{1,0:T(8,128)(2,1)S(1)}, bf16[8,128]{1,0:T(8,128)(2,1)S(1)}, u32[]{:S(2)}, u32[]{:S(2)}) collective-permute-start(bf16[8,128]{1,0:T(8,128)(2,1)S(1)} %get-tuple-element.76), channel_id=1, source_target_pairs={{1,0},{3,2},{5,4},{7,6},{9,8},{11,10},{13,12},{15,14},{17,16},{19,... | collective-permute-start | bytes 6152 | tf_op jit(solution)/shard_map/ppermute | solution.py:30
  342.0 0.7 copy-start.2
Sparse Core Ops, SparseCore 0:
  37.4 38.2 all-gather.4
  77.8 36.8 all-gather.6
  342.1 63.1 all-reduce.4
